TPU v7x, 32 devices: a whole 2x2x4 slice. The times are simulated.
32 devices in a mesh: row: 16 (over z, y, core), col: 2 (over x).
Axes of the slice: x: 2, y: 2, z: 4, core: 2. Of those that a mesh axis runs over, the one named last changes fastest.
Arguments:
- vectors: float32 [32, 65536], P(None, ('row', 'col')), may hold values from -6 to 6
- block_values: bfloat16 [8192, 128, 128], P(('row', 'col')), may hold values from -0.15625 to 0.15625
- block_rows: int32 [8192], P(('row', 'col')), may hold values from 0 to 31, as said below
- block_cols: int32 [8192], P(('row', 'col')), may hold values from 0 to 255, as said below
- block_counts: int32 [32], P(('row', 'col')), may hold values from 32 to 256, as said below
- center: float32 [1], replicated, may hold values from -0.5 to 0.5
- radius: float32 [1], replicated, may hold values from 1.5 to 3
Outputs:
- filtered: float32 [32, 65536], P(None, ('row', 'col'))
Inputs may be any that keep to these rules, and one draw needn't show every extreme that they name: `block_counts`: live slots of each device; some device fills all 256 slots. `block_rows`: Block-row inside the row group; slots may repeat a position. `block_cols`: Block-column inside the col group; slots may repeat a position.
All inputs are finite; a program needn't handle non-finite values.
Results may differ from a plain program's by a relative error of at most 0.02.
Values may be sent and summed in bfloat16 or wider, within the bound.
No kernel may reach another device: no remote copies, remote signals or barrier semaphores. Data moves between devices by JAX's collectives and lax.ppermute only.
A program may use at most 128 MiB of HBM per device.

v0:
```python
import functools

import jax
import jax.numpy as jnp
from jax import lax
from jax.experimental import pallas as pl
from jax.experimental.pallas import tpu as pltpu
from jax.sharding import PartitionSpec as P

CHUNK = 32
UNROLL = 8


def product_kernel(contract, outputs, n_in, count_ref, take_ref, put_ref, *refs):
    pieces = refs[:n_in]
    blocks = refs[n_in]
    outs = refs[n_in + 1 : n_in + 1 + len(outputs)]
    held, held_blocks, total, piece_sems, block_sems = refs[n_in + 1 + len(outputs) :]
    capacity, size_block = blocks.shape[0], blocks.shape[1]
    per_piece = held.shape[2] // size_block
    chunks = capacity // CHUNK
    count = count_ref[0]

    copies = [pltpu.make_async_copy(pieces[p], held.at[p], piece_sems.at[p]) for p in range(n_in)]
    for copy in copies:
        copy.start()

    def block_copy(g):
        part = pl.ds(g * CHUNK, CHUNK)
        return pltpu.make_async_copy(blocks.at[part], held_blocks.at[part], block_sems.at[g])

    for g in range(chunks):
        @pl.when(g * CHUNK < count)
        def _(g=g):
            block_copy(g).start()

    total[...] = jnp.zeros_like(total)
    for copy in copies:
        copy.wait()

    def group(first):
        places = []
        sums = []
        for n in range(UNROLL):
            slot = first + n
            take = take_ref[slot]
            put = put_ref[slot]
            column = pl.multiple_of((take % per_piece) * size_block, size_block)
            picked = held[take // per_piece, :, pl.ds(column, size_block)]
            sums.append(
                lax.dot_general(
                    picked, held_blocks[slot], (((1,), (contract,)), ((), ())), preferred_element_type=jnp.float32
                )
            )
            column = pl.multiple_of((put % per_piece) * size_block, size_block)
            places.append((put // per_piece, slice(None), pl.ds(column, size_block)))
        for place, value in zip(places, sums):
            total[place] += value

    for g in range(chunks):
        @pl.when(g * CHUNK < count)
        def _(g=g):
            block_copy(g).wait()

            @pl.loop(0, CHUNK // UNROLL)
            def _(n):
                group(g * CHUNK + n * UNROLL)

    for out, held_pieces in zip(outs, outputs):
        for n, p in enumerate(held_pieces):
            out[n] = total[p].astype(out.dtype)


def block_product(contract, outputs, dtypes, n_put, count, take, put, pieces, blocks):
    capacity, size_block = blocks.shape[0], blocks.shape[1]
    vector_count, own_rows = pieces[0].shape
    n_in = len(pieces)
    smem = pl.BlockSpec(memory_space=pltpu.SMEM)
    anywhere = pl.BlockSpec(memory_space=pl.ANY)
    return pl.pallas_call(
        functools.partial(product_kernel, contract, outputs, n_in),
        out_shape=[
            jax.ShapeDtypeStruct((len(held), vector_count, own_rows), dtype) for held, dtype in zip(outputs, dtypes)
        ],
        in_specs=[smem] * 3 + [anywhere] * (n_in + 1),
        out_specs=[pl.BlockSpec(memory_space=pltpu.VMEM)] * len(outputs),
        scratch_shapes=[
            pltpu.VMEM((n_in, vector_count, own_rows), jnp.bfloat16),
            pltpu.VMEM(blocks.shape, blocks.dtype),
            pltpu.VMEM((n_put + 1, vector_count, own_rows), jnp.float32),
            pltpu.SemaphoreType.DMA((n_in,)),
            pltpu.SemaphoreType.DMA((capacity // CHUNK,)),
        ],
        compiler_params=pltpu.CompilerParams(vmem_limit_bytes=40 * 1024 * 1024),
        cost_estimate=pl.CostEstimate(
            flops=2 * capacity * size_block * size_block * 256,
            bytes_accessed=2 * blocks.size + 2 * n_in * vector_count * own_rows,
            transcendentals=0,
        ),
        name="mirror" if contract == 0 else "forward",
    )(count, take, put, *pieces, blocks)


def shards(n_row, n_col, vectors, block_values, block_rows, block_cols, block_counts, center, radius):
    size_block = block_values.shape[1]
    own_rows = vectors.shape[1]
    per_piece = own_rows // size_block
    center_value = center[0]
    radius_value = radius[0]

    n_c = 2 if n_row % 2 == 0 else 1
    n_a = 4 if (n_row // n_c) % 4 == 0 else n_row // n_c
    n_b = n_row // n_c // n_a

    def at(a, b, c):
        return ((a % n_a) * n_b + b % n_b) * n_c + c % n_c

    spots = [(a, b, c) for a in range(n_a) for b in range(n_b) for c in range(n_c)]

    def shift(value, da=0, db=0, dc=0):
        pairs = [(at(a, b, c), at(a + da, b + db, c + dc)) for a, b, c in spots]
        return lax.ppermute(value, "row", pairs)

    def shift_col(value, d):
        return lax.ppermute(value, "col", [(j, (j + d) % n_col) for j in range(n_col)])

    row_index = lax.axis_index("row").astype(jnp.int32)
    col_index = lax.axis_index("col").astype(jnp.int32)
    my_c, my_b, my_a = row_index % n_c, row_index // n_c % n_b, row_index // (n_c * n_b)

    def piece(da, db, dc):
        return (dc * n_b + db) * n_a + da

    owner = block_cols // per_piece
    owner_c, owner_b, owner_a = owner % n_c, owner // n_c % n_b, owner // (n_c * n_b)
    place_cols = (
        piece((my_a - owner_a + n_a) % n_a, (my_b - owner_b + n_b) % n_b, (my_c - owner_c + n_c) % n_c) * per_piece
        + block_cols % per_piece
    )
    place_rows = (col_index - block_rows // per_piece + n_col) % n_col * per_piece + block_rows % per_piece
    live = jnp.arange(block_rows.shape[0], dtype=jnp.int32) < block_counts[0]
    put_cols = jnp.where(live, place_cols, n_row * per_piece)
    put_rows = jnp.where(live, place_rows, n_col * per_piece)

    mirror_outputs = [
        [piece(a, b, c) for a in range(n_a)] for c in range(n_c) for b in range(n_b)
    ]
    forward_outputs = [[j] for j in range(n_col)]

    def apply_operator(narrow):
        by_col = [narrow] + [shift_col(narrow, j) for j in range(1, n_col)]
        along_a = [narrow] + [shift(narrow, da=a) for a in range(1, n_a)]
        mirrors = block_product(
            0, mirror_outputs, [jnp.bfloat16] * len(mirror_outputs), n_row,
            block_counts, place_rows, put_cols, by_col, block_values,
        )
        along_a, mirrors = lax.optimization_barrier((along_a, mirrors))
        along_b = list(along_a)
        for b in range(1, n_b):
            along_b += [shift(part, db=b) for part in along_a]
        by_row = list(along_b)
        for c in range(1, n_c):
            by_row += [shift(part, dc=c) for part in along_b]

        by_b = []
        for b in range(n_b):
            share = mirrors[b].astype(jnp.float32)
            for c in range(1, n_c):
                share += shift(mirrors[c * n_b + b], dc=-c).astype(jnp.float32)
            by_b.append(share)
        share = by_b[0]
        for b in range(1, n_b):
            share += shift(by_b[b].astype(jnp.bfloat16), db=-b).astype(jnp.float32)
        mirror_sum = share[0]
        for a in range(1, n_a):
            mirror_sum += shift(share[a].astype(jnp.bfloat16), da=-a).astype(jnp.float32)

        forwards = block_product(
            1, forward_outputs, [jnp.float32] + [jnp.bfloat16] * (n_col - 1), n_col,
            block_counts, place_cols, put_rows, by_row, block_values,
        )
        forward_sum = forwards[0][0]
        for j in range(1, n_col):
            forward_sum += shift_col(forwards[j][0], -j).astype(jnp.float32)
        return forward_sum + mirror_sum

    current = (apply_operator(vectors.astype(jnp.bfloat16)) - center_value * vectors) / radius_value
    return 2.0 * (apply_operator(current.astype(jnp.bfloat16)) - center_value * current) / radius_value - vectors


def solution(mesh):
    return jax.shard_map(
        functools.partial(shards, mesh.shape["row"], mesh.shape["col"]),
        mesh=mesh,
        in_specs=(
            P(None, ("row", "col")),
            P(("row", "col"), None, None),
            P(("row", "col")),
            P(("row", "col")),
            P(("row", "col")),
            P(),
            P(),
        ),
        out_specs=P(None, ("row", "col")),
        check_vma=False,
    )
```

profile of v0, /device:TPU:9, one launch (start us, length us, event | category | flops | bytes accessed | tf_op | source)
XLA Modules:
  0.0 127.9 jit_solution(7462045075186289064)
XLA Ops:
  3.4 1.4 %collective-permute-start.2 = (bf16[32,2048]{1,0:T(8,128)(2,1)S(1)}, bf16[32,2048]{1,0:T(8,128)(2,1)S(1)}, u32[]{:S(2)}, u32[]{:S(2)}) collective-permute-start(bf16[32,2048]{1,0:T(8,128)(2,1)S(1)} %convert_element_type.90.refs_0_), channel_id=1, source_target_pairs={{0,24},{2,26},{4,28},{6,30},{8,0},{10,2},{12,4},{14,6},{16,8},{18,... | collective-permute-start | bytes 393224 | tf_op jit(solution)/shard_map/ppermute | solution.py:122
  7.4 1.5 %collective-permute-done.3.refs_1_ = bf16[32,2048]{1,0:T(8,128)(2,1)S(1)} collective-permute-done((bf16[32,2048]{1,0:T(8,128)(2,1)S(1)}, bf16[32,2048]{1,0:T(8,128)(2,1)S(1)}, u32[]{:S(2)}, u32[]{:S(2)}) %collective-permute-start.3) | collective-permute-done | bytes 131104 | tf_op jit(solution)/shard_map/ppermute | solution.py:125
  8.9 3.4 %copy-done = bf16[256,128,128]{2,1,0:T(8,128)(2,1)S(1)} copy-done((bf16[256,128,128]{2,1,0:T(8,128)(2,1)S(1)}, bf16[256,128,128]{2,1,0:T(8,128)(2,1)}, u32[]{:S(2)}) %copy-start) | copy-done | bytes 8388632
  12.3 4.1 %mirror.2 = (bf16[4,32,2048]{2,1,0:T(8,128)(2,1)S(1)}, bf16[4,32,2048]{2,1,0:T(8,128)(2,1)S(1)}, bf16[4,32,2048]{2,1,0:T(8,128)(2,1)S(1)}, bf16[4,32,2048]{2,1,0:T(8,128)(2,1)S(1)}) custom-call(s32[1]{0:T(128)} %copy.8.count_ref, s32[256]{0:T(256)S(1)} %get-tuple-element.78.take_ref, s32[256]{0:T(256)S(1)} %get-tuple-element.69.put_ref, ...), custom_call_target="tpu_custom_call" | custom-call | flops 2147483648 | bytes 8650752 | tf_op jit(solution)/shard_map/mirror/pallas_call | solution.py:80
  17.2 7.1 %collective-permute-start.4 = (bf16[32,2048]{1,0:T(8,128)(2,1)S(1)}, bf16[32,2048]{1,0:T(8,128)(2,1)S(1)}, u32[]{:S(2)}, u32[]{:S(2)}) collective-permute-start(bf16[32,2048]{1,0:T(8,128)(2,1)S(1)} %convert_element_type.90.refs_0_), channel_id=1, source_target_pairs={{0,4},{2,6},{4,0},{6,2},{8,12},{10,14},{12,8},{14,10},{16,20},{18,... | collective-permute-start | bytes 393224 | tf_op jit(solution)/shard_map/ppermute | solution.py:122
  25.0 3.0 %collective-permute-done.4.refs_4_ = bf16[32,2048]{1,0:T(8,128)(2,1)S(1)} collective-permute-done((bf16[32,2048]{1,0:T(8,128)(2,1)S(1)}, bf16[32,2048]{1,0:T(8,128)(2,1)S(1)}, u32[]{:S(2)}, u32[]{:S(2)}) %collective-permute-start.4) | collective-permute-done | bytes 131104 | tf_op jit(solution)/shard_map/ppermute | solution.py:122
  34.1 1.5 %collective-permute-done.7.refs_7_ = bf16[32,2048]{1,0:T(8,128)(2,1)S(1)} collective-permute-done((bf16[32,2048]{1,0:T(8,128)(2,1)S(1)}, bf16[32,2048]{1,0:T(8,128)(2,1)S(1)}, u32[]{:S(2)}, u32[]{:S(2)}) %collective-permute-start.7) | collective-permute-done | bytes 131104 | tf_op jit(solution)/shard_map/ppermute | solution.py:122
  35.6 2.6 %collective-permute-start.10 = (bf16[32,2048]{1,0:T(8,128)(2,1)S(1)}, bf16[32,2048]{1,0:T(8,128)(2,1)S(1)}, u32[]{:S(2)}, u32[]{:S(2)}) collective-permute-start(bf16[32,2048]{1,0:T(8,128)(2,1)S(1)} %collective-permute-done.1.refs_2_), channel_id=1, source_target_pairs={{0,2},{2,0},{4,6},{6,4},{8,10},{10,8},{12,14},{14,12},{16,18},{18,... | collective-permute-start | bytes 393224 | tf_op jit(solution)/shard_map/ppermute | solution.py:122
  41.1 7.1 %forward.2 = (f32[1,32,2048]{2,1,0:T(8,128)S(1)}, bf16[1,32,2048]{2,1,0:T(8,128)(2,1)S(1)}) custom-call(s32[1]{0:T(128)} %copy.8.count_ref, s32[256]{0:T(256)S(1)} %get-tuple-element.70.take_ref, s32[256]{0:T(256)S(1)} %get-tuple-element.77.put_ref, bf16[32,2048]{1,0:T(8,128)(2,1)S(1)} %convert_element_type.90.refs_0_, ...), custom_call_target="tpu_custom_call" | custom-call | flops 2147483648 | bytes 10485760 | tf_op jit(solution)/shard_map/forward/pallas_call | solution.py:80
  48.1 6.8 %collective-permute-start.16 = (bf16[32,2048]{1,0:T(8,128)(2,1)S(1)}, bf16[32,2048]{1,0:T(8,128)(2,1)S(1)}, u32[]{:S(2)}, u32[]{:S(2)}) collective-permute-start(bf16[32,2048]{1,0:T(8,128)(2,1)S(1)} %bitcast.65), channel_id=1, source_target_pairs={{0,1},{1,0},{2,3},{3,2},{4,5},{5,4},{6,7},{7,6},{8,9},{9,8},{10,11... | collective-permute-start | bytes 393224 | tf_op jit(solution)/shard_map/ppermute | solution.py:125
  59.2 7.0 %collective-permute-done.21 = bf16[32,2048]{1,0:T(8,128)(2,1)S(1)} collective-permute-done((bf16[32,2048]{1,0:T(8,128)(2,1)S(1)}, bf16[32,2048]{1,0:T(8,128)(2,1)S(1)}, u32[]{:S(2)}, u32[]{:S(2)}) %collective-permute-start.21) | collective-permute-done | bytes 131104 | tf_op jit(solution)/shard_map/ppermute | solution.py:122
  66.8 3.1 %collective-permute-start.24 = (bf16[32,2048]{1,0:T(8,128)(2,1)S(1)}, bf16[32,2048]{1,0:T(8,128)(2,1)S(1)}, u32[]{:S(2)}, u32[]{:S(2)}) collective-permute-start(bf16[32,2048]{1,0:T(8,128)(2,1)S(1)} %get-tuple-element.51.refs_0_), channel_id=1, source_target_pairs={{0,16},{2,18},{4,20},{6,22},{8,24},{10,26},{12,28},{14,30},{16,0},... | collective-permute-start | bytes 393224 | tf_op jit(solution)/shard_map/ppermute | solution.py:122
  69.9 1.5 %collective-permute-start.25 = (bf16[32,2048]{1,0:T(8,128)(2,1)S(1)}, bf16[32,2048]{1,0:T(8,128)(2,1)S(1)}, u32[]{:S(2)}, u32[]{:S(2)}) collective-permute-start(bf16[32,2048]{1,0:T(8,128)(2,1)S(1)} %get-tuple-element.51.refs_0_), channel_id=1, source_target_pairs={{0,24},{2,26},{4,28},{6,30},{8,0},{10,2},{12,4},{14,6},{16,8},{18,... | collective-permute-start | bytes 393224 | tf_op jit(solution)/shard_map/ppermute | solution.py:122
  71.3 4.1 %mirror.3 = (bf16[4,32,2048]{2,1,0:T(8,128)(2,1)S(1)}, bf16[4,32,2048]{2,1,0:T(8,128)(2,1)S(1)}, bf16[4,32,2048]{2,1,0:T(8,128)(2,1)S(1)}, bf16[4,32,2048]{2,1,0:T(8,128)(2,1)S(1)}) custom-call(s32[1]{0:T(128)} %copy.8.count_ref, s32[256]{0:T(256)S(1)} %get-tuple-element.78.take_ref, s32[256]{0:T(256)S(1)} %get-tuple-element.69.put_ref, ...), custom_call_target="tpu_custom_call" | custom-call | flops 2147483648 | bytes 8650752 | tf_op jit(solution)/shard_map/mirror/pallas_call | solution.py:80
  75.4 2.6 %collective-permute-done.24.refs_2_ = bf16[32,2048]{1,0:T(8,128)(2,1)S(1)} collective-permute-done((bf16[32,2048]{1,0:T(8,128)(2,1)S(1)}, bf16[32,2048]{1,0:T(8,128)(2,1)S(1)}, u32[]{:S(2)}, u32[]{:S(2)}) %collective-permute-start.24) | collective-permute-done | bytes 131104 | tf_op jit(solution)/shard_map/ppermute | solution.py:122
  78.0 4.3 %collective-permute-done.25.refs_3_ = bf16[32,2048]{1,0:T(8,128)(2,1)S(1)} collective-permute-done((bf16[32,2048]{1,0:T(8,128)(2,1)S(1)}, bf16[32,2048]{1,0:T(8,128)(2,1)S(1)}, u32[]{:S(2)}, u32[]{:S(2)}) %collective-permute-start.25) | collective-permute-done | bytes 131104 | tf_op jit(solution)/shard_map/ppermute | solution.py:122
  82.7 2.7 %collective-permute-start.27 = (bf16[32,2048]{1,0:T(8,128)(2,1)S(1)}, bf16[32,2048]{1,0:T(8,128)(2,1)S(1)}, u32[]{:S(2)}, u32[]{:S(2)}) collective-permute-start(bf16[32,2048]{1,0:T(8,128)(2,1)S(1)} %get-tuple-element.51.refs_0_), channel_id=1, source_target_pairs={{0,4},{2,6},{4,0},{6,2},{8,12},{10,14},{12,8},{14,10},{16,20},{18,... | collective-permute-start | bytes 393224 | tf_op jit(solution)/shard_map/ppermute | solution.py:122
  86.3 3.0 %collective-permute-done.27.refs_4_ = bf16[32,2048]{1,0:T(8,128)(2,1)S(1)} collective-permute-done((bf16[32,2048]{1,0:T(8,128)(2,1)S(1)}, bf16[32,2048]{1,0:T(8,128)(2,1)S(1)}, u32[]{:S(2)}, u32[]{:S(2)}) %collective-permute-start.27) | collective-permute-done | bytes 131104 | tf_op jit(solution)/shard_map/ppermute | solution.py:122
  95.3 1.5 %collective-permute-done.30.refs_7_ = bf16[32,2048]{1,0:T(8,128)(2,1)S(1)} collective-permute-done((bf16[32,2048]{1,0:T(8,128)(2,1)S(1)}, bf16[32,2048]{1,0:T(8,128)(2,1)S(1)}, u32[]{:S(2)}, u32[]{:S(2)}) %collective-permute-start.30) | collective-permute-done | bytes 131104 | tf_op jit(solution)/shard_map/ppermute | solution.py:122
  96.9 2.6 %collective-permute-start.33 = (bf16[32,2048]{1,0:T(8,128)(2,1)S(1)}, bf16[32,2048]{1,0:T(8,128)(2,1)S(1)}, u32[]{:S(2)}, u32[]{:S(2)}) collective-permute-start(bf16[32,2048]{1,0:T(8,128)(2,1)S(1)} %collective-permute-done.24.refs_2_), channel_id=1, source_target_pairs={{0,2},{2,0},{4,6},{6,4},{8,10},{10,8},{12,14},{14,12},{16,18},{18,... | collective-permute-start | bytes 393224 | tf_op jit(solution)/shard_map/ppermute | solution.py:122
  102.3 7.1 %forward.3 = (f32[1,32,2048]{2,1,0:T(8,128)S(1)}, bf16[1,32,2048]{2,1,0:T(8,128)(2,1)S(1)}) custom-call(s32[1]{0:T(128)} %copy.8.count_ref, s32[256]{0:T(256)S(1)} %get-tuple-element.70.take_ref, s32[256]{0:T(256)S(1)} %get-tuple-element.77.put_ref, bf16[32,2048]{1,0:T(8,128)(2,1)S(1)} %get-tuple-element.51.refs_0_, ...), custom_call_target="tpu_custom_call" | custom-call | flops 2147483648 | bytes 10485760 | tf_op jit(solution)/shard_map/forward/pallas_call | solution.py:80
  109.4 5.7 %collective-permute-start.39 = (bf16[32,2048]{1,0:T(8,128)(2,1)S(1)}, bf16[32,2048]{1,0:T(8,128)(2,1)S(1)}, u32[]{:S(2)}, u32[]{:S(2)}) collective-permute-start(bf16[32,2048]{1,0:T(8,128)(2,1)S(1)} %bitcast.64), channel_id=1, source_target_pairs={{0,1},{1,0},{2,3},{3,2},{4,5},{5,4},{6,7},{7,6},{8,9},{9,8},{10,11... | collective-permute-start | bytes 393224 | tf_op jit(solution)/shard_map/ppermute | solution.py:125
  117.5 3.5 %collective-permute-done.45 = bf16[32,2048]{1,0:T(8,128)(2,1)S(1)} collective-permute-done((bf16[32,2048]{1,0:T(8,128)(2,1)S(1)}, bf16[32,2048]{1,0:T(8,128)(2,1)S(1)}, u32[]{:S(2)}, u32[]{:S(2)}) %collective-permute-start.45) | collective-permute-done | bytes 131104 | tf_op jit(solution)/shard_map/ppermute | solution.py:122
  121.0 6.0 %collective-permute-done.44 = bf16[32,2048]{1,0:T(8,128)(2,1)S(1)} collective-permute-done((bf16[32,2048]{1,0:T(8,128)(2,1)S(1)}, bf16[32,2048]{1,0:T(8,128)(2,1)S(1)}, u32[]{:S(2)}, u32[]{:S(2)}) %collective-permute-start.44) | collective-permute-done | bytes 131104 | tf_op jit(solution)/shard_map/ppermute | solution.py:122
  (88 shorter events, 32.8 us)
Async XLA Ops:
  1.0 15.4 %collective-permute-start = (bf16[32,2048]{1,0:T(8,128)(2,1)S(1)}, bf16[32,2048]{1,0:T(8,128)(2,1)S(1)}, u32[]{:S(2)}, u32[]{:S(2)}) collective-permute-start(bf16[32,2048]{1,0:T(8,128)(2,1)S(1)} %convert_element_type.90.refs_0_), channel_id=1, source_target_pairs={{0,8},{2,10},{4,12},{6,14},{8,16},{10,18},{12,20},{14,22},{16,24},... | collective-permute-start | bytes 393224 | tf_op jit(solution)/shard_map/ppermute | solution.py:122
  2.3 14.1 %collective-permute-start.1 = (bf16[32,2048]{1,0:T(8,128)(2,1)S(1)}, bf16[32,2048]{1,0:T(8,128)(2,1)S(1)}, u32[]{:S(2)}, u32[]{:S(2)}) collective-permute-start(bf16[32,2048]{1,0:T(8,128)(2,1)S(1)} %convert_element_type.90.refs_0_), channel_id=1, source_target_pairs={{0,16},{2,18},{4,20},{6,22},{8,24},{10,26},{12,28},{14,30},{16,0},... | collective-permute-start | bytes 393224 | tf_op jit(solution)/shard_map/ppermute | solution.py:122
  3.4 13.0 %collective-permute-start.2 = (bf16[32,2048]{1,0:T(8,128)(2,1)S(1)}, bf16[32,2048]{1,0:T(8,128)(2,1)S(1)}, u32[]{:S(2)}, u32[]{:S(2)}) collective-permute-start(bf16[32,2048]{1,0:T(8,128)(2,1)S(1)} %convert_element_type.90.refs_0_), channel_id=1, source_target_pairs={{0,24},{2,26},{4,28},{6,30},{8,0},{10,2},{12,4},{14,6},{16,8},{18,... | collective-permute-start | bytes 393224 | tf_op jit(solution)/shard_map/ppermute | solution.py:122
  16.4 12.9 %collective-permute-start.18 = (bf16[4,32,2048]{2,1,0:T(8,128)(2,1)S(1)}, bf16[4,32,2048]{2,1,0:T(8,128)(2,1)S(1)}, u32[]{:S(2)}, u32[]{:S(2)}) collective-permute-start(bf16[4,32,2048]{2,1,0:T(8,128)(2,1)S(1)} %get-tuple-element.46), channel_id=1, source_target_pairs={{0,2},{2,0},{4,6},{6,4},{8,10},{10,8},{12,14},{14,12},{16,18},{18,... | collective-permute-start | bytes 1572872 | tf_op jit(solution)/shard_map/ppermute | solution.py:122
  17.2 10.9 %collective-permute-start.4 = (bf16[32,2048]{1,0:T(8,128)(2,1)S(1)}, bf16[32,2048]{1,0:T(8,128)(2,1)S(1)}, u32[]{:S(2)}, u32[]{:S(2)}) collective-permute-start(bf16[32,2048]{1,0:T(8,128)(2,1)S(1)} %convert_element_type.90.refs_0_), channel_id=1, source_target_pairs={{0,4},{2,6},{4,0},{6,2},{8,12},{10,14},{12,8},{14,10},{16,20},{18,... | collective-permute-start | bytes 393224 | tf_op jit(solution)/shard_map/ppermute | solution.py:122
  24.2 13.9 %collective-permute-start.8 = (bf16[32,2048]{1,0:T(8,128)(2,1)S(1)}, bf16[32,2048]{1,0:T(8,128)(2,1)S(1)}, u32[]{:S(2)}, u32[]{:S(2)}) collective-permute-start(bf16[32,2048]{1,0:T(8,128)(2,1)S(1)} %convert_element_type.90.refs_0_), channel_id=1, source_target_pairs={{0,2},{2,0},{4,6},{6,4},{8,10},{10,8},{12,14},{14,12},{16,18},{18,... | collective-permute-start | bytes 393224 | tf_op jit(solution)/shard_map/ppermute | solution.py:122
  24.6 13.6 %collective-permute-start.9 = (bf16[32,2048]{1,0:T(8,128)(2,1)S(1)}, bf16[32,2048]{1,0:T(8,128)(2,1)S(1)}, u32[]{:S(2)}, u32[]{:S(2)}) collective-permute-start(bf16[32,2048]{1,0:T(8,128)(2,1)S(1)} %collective-permute-done.refs_1_), channel_id=1, source_target_pairs={{0,2},{2,0},{4,6},{6,4},{8,10},{10,8},{12,14},{14,12},{16,18},{18,... | collective-permute-start | bytes 393224 | tf_op jit(solution)/shard_map/ppermute | solution.py:122
  30.8 24.1 %collective-permute-start.17 = (bf16[4,32,2048]{2,1,0:T(8,128)(2,1)S(1)}, bf16[4,32,2048]{2,1,0:T(8,128)(2,1)S(1)}, u32[]{:S(2)}, u32[]{:S(2)}) collective-permute-start(bf16[4,32,2048]{2,1,0:T(8,128)(2,1)S(1)} %get-tuple-element.44), channel_id=1, source_target_pairs={{0,2},{2,0},{4,6},{6,4},{8,10},{10,8},{12,14},{14,12},{16,18},{18,... | collective-permute-start | bytes 1572872 | tf_op jit(solution)/shard_map/ppermute | solution.py:122
  32.8 22.1 %collective-permute-start.19 = (bf16[4,32,2048]{2,1,0:T(8,128)(2,1)S(1)}, bf16[4,32,2048]{2,1,0:T(8,128)(2,1)S(1)}, u32[]{:S(2)}, u32[]{:S(2)}) collective-permute-start(bf16[4,32,2048]{2,1,0:T(8,128)(2,1)S(1)} %add_convert_fusion.1), channel_id=1, source_target_pairs={{0,4},{2,6},{4,0},{6,2},{8,12},{10,14},{12,8},{14,10},{16,20},{18,... | collective-permute-start | bytes 1572872 | tf_op jit(solution)/shard_map/ppermute | solution.py:122
  48.1 10.0 %collective-permute-start.16 = (bf16[32,2048]{1,0:T(8,128)(2,1)S(1)}, bf16[32,2048]{1,0:T(8,128)(2,1)S(1)}, u32[]{:S(2)}, u32[]{:S(2)}) collective-permute-start(bf16[32,2048]{1,0:T(8,128)(2,1)S(1)} %bitcast.65), channel_id=1, source_target_pairs={{0,1},{1,0},{2,3},{3,2},{4,5},{5,4},{6,7},{7,6},{8,9},{9,8},{10,11... | collective-permute-start | bytes 393224 | tf_op jit(solution)/shard_map/ppermute | solution.py:125
  55.6 10.7 %collective-permute-start.21 = (bf16[32,2048]{1,0:T(8,128)(2,1)S(1)}, bf16[32,2048]{1,0:T(8,128)(2,1)S(1)}, u32[]{:S(2)}, u32[]{:S(2)}) collective-permute-start(bf16[32,2048]{1,0:T(8,128)(2,1)S(1)} %get-tuple-element.76), channel_id=1, source_target_pairs={{0,16},{2,18},{4,20},{6,22},{8,24},{10,26},{12,28},{14,30},{16,0},... | collective-permute-start | bytes 393224 | tf_op jit(solution)/shard_map/ppermute | solution.py:122
  55.6 10.7 %collective-permute-start.20 = (bf16[32,2048]{1,0:T(8,128)(2,1)S(1)}, bf16[32,2048]{1,0:T(8,128)(2,1)S(1)}, u32[]{:S(2)}, u32[]{:S(2)}) collective-permute-start(bf16[32,2048]{1,0:T(8,128)(2,1)S(1)} %get-tuple-element.74), channel_id=1, source_target_pairs={{0,24},{2,26},{4,28},{6,30},{8,0},{10,2},{12,4},{14,6},{16,8},{18,... | collective-permute-start | bytes 393224 | tf_op jit(solution)/shard_map/ppermute | solution.py:122
  66.8 8.6 %collective-permute-start.23 = (bf16[32,2048]{1,0:T(8,128)(2,1)S(1)}, bf16[32,2048]{1,0:T(8,128)(2,1)S(1)}, u32[]{:S(2)}, u32[]{:S(2)}) collective-permute-start(bf16[32,2048]{1,0:T(8,128)(2,1)S(1)} %get-tuple-element.51.refs_0_), channel_id=1, source_target_pairs={{0,8},{2,10},{4,12},{6,14},{8,16},{10,18},{12,20},{14,22},{16,24},... | collective-permute-start | bytes 393224 | tf_op jit(solution)/shard_map/ppermute | solution.py:122
  66.8 11.2 %collective-permute-start.24 = (bf16[32,2048]{1,0:T(8,128)(2,1)S(1)}, bf16[32,2048]{1,0:T(8,128)(2,1)S(1)}, u32[]{:S(2)}, u32[]{:S(2)}) collective-permute-start(bf16[32,2048]{1,0:T(8,128)(2,1)S(1)} %get-tuple-element.51.refs_0_), channel_id=1, source_target_pairs={{0,16},{2,18},{4,20},{6,22},{8,24},{10,26},{12,28},{14,30},{16,0},... | collective-permute-start | bytes 393224 | tf_op jit(solution)/shard_map/ppermute | solution.py:122
  69.9 12.4 %collective-permute-start.25 = (bf16[32,2048]{1,0:T(8,128)(2,1)S(1)}, bf16[32,2048]{1,0:T(8,128)(2,1)S(1)}, u32[]{:S(2)}, u32[]{:S(2)}) collective-permute-start(bf16[32,2048]{1,0:T(8,128)(2,1)S(1)} %get-tuple-element.51.refs_0_), channel_id=1, source_target_pairs={{0,24},{2,26},{4,28},{6,30},{8,0},{10,2},{12,4},{14,6},{16,8},{18,... | collective-permute-start | bytes 393224 | tf_op jit(solution)/shard_map/ppermute | solution.py:122
  82.2 8.3 %collective-permute-start.41 = (bf16[4,32,2048]{2,1,0:T(8,128)(2,1)S(1)}, bf16[4,32,2048]{2,1,0:T(8,128)(2,1)S(1)}, u32[]{:S(2)}, u32[]{:S(2)}) collective-permute-start(bf16[4,32,2048]{2,1,0:T(8,128)(2,1)S(1)} %get-tuple-element.60), channel_id=1, source_target_pairs={{0,2},{2,0},{4,6},{6,4},{8,10},{10,8},{12,14},{14,12},{16,18},{18,... | collective-permute-start | bytes 1572872 | tf_op jit(solution)/shard_map/ppermute | solution.py:122
  82.7 6.5 %collective-permute-start.27 = (bf16[32,2048]{1,0:T(8,128)(2,1)S(1)}, bf16[32,2048]{1,0:T(8,128)(2,1)S(1)}, u32[]{:S(2)}, u32[]{:S(2)}) collective-permute-start(bf16[32,2048]{1,0:T(8,128)(2,1)S(1)} %get-tuple-element.51.refs_0_), channel_id=1, source_target_pairs={{0,4},{2,6},{4,0},{6,2},{8,12},{10,14},{12,8},{14,10},{16,20},{18,... | collective-permute-start | bytes 393224 | tf_op jit(solution)/shard_map/ppermute | solution.py:122
  85.5 13.9 %collective-permute-start.31 = (bf16[32,2048]{1,0:T(8,128)(2,1)S(1)}, bf16[32,2048]{1,0:T(8,128)(2,1)S(1)}, u32[]{:S(2)}, u32[]{:S(2)}) collective-permute-start(bf16[32,2048]{1,0:T(8,128)(2,1)S(1)} %get-tuple-element.51.refs_0_), channel_id=1, source_target_pairs={{0,2},{2,0},{4,6},{6,4},{8,10},{10,8},{12,14},{14,12},{16,18},{18,... | collective-permute-start | bytes 393224 | tf_op jit(solution)/shard_map/ppermute | solution.py:122
  85.8 13.6 %collective-permute-start.32 = (bf16[32,2048]{1,0:T(8,128)(2,1)S(1)}, bf16[32,2048]{1,0:T(8,128)(2,1)S(1)}, u32[]{:S(2)}, u32[]{:S(2)}) collective-permute-start(bf16[32,2048]{1,0:T(8,128)(2,1)S(1)} %collective-permute-done.23.refs_1_), channel_id=1, source_target_pairs={{0,2},{2,0},{4,6},{6,4},{8,10},{10,8},{12,14},{14,12},{16,18},{18,... | collective-permute-start | bytes 393224 | tf_op jit(solution)/shard_map/ppermute | solution.py:122
  92.1 23.1 %collective-permute-start.40 = (bf16[4,32,2048]{2,1,0:T(8,128)(2,1)S(1)}, bf16[4,32,2048]{2,1,0:T(8,128)(2,1)S(1)}, u32[]{:S(2)}, u32[]{:S(2)}) collective-permute-start(bf16[4,32,2048]{2,1,0:T(8,128)(2,1)S(1)} %get-tuple-element.58), channel_id=1, source_target_pairs={{0,2},{2,0},{4,6},{6,4},{8,10},{10,8},{12,14},{14,12},{16,18},{18,... | collective-permute-start | bytes 1572872 | tf_op jit(solution)/shard_map/ppermute | solution.py:122
  94.0 21.1 %collective-permute-start.42 = (bf16[4,32,2048]{2,1,0:T(8,128)(2,1)S(1)}, bf16[4,32,2048]{2,1,0:T(8,128)(2,1)S(1)}, u32[]{:S(2)}, u32[]{:S(2)}) collective-permute-start(bf16[4,32,2048]{2,1,0:T(8,128)(2,1)S(1)} %add_convert_fusion), channel_id=1, source_target_pairs={{0,4},{2,6},{4,0},{6,2},{8,12},{10,14},{12,8},{14,10},{16,20},{18,... | collective-permute-start | bytes 1572872 | tf_op jit(solution)/shard_map/ppermute | solution.py:122
  109.4 8.1 %collective-permute-start.39 = (bf16[32,2048]{1,0:T(8,128)(2,1)S(1)}, bf16[32,2048]{1,0:T(8,128)(2,1)S(1)}, u32[]{:S(2)}, u32[]{:S(2)}) collective-permute-start(bf16[32,2048]{1,0:T(8,128)(2,1)S(1)} %bitcast.64), channel_id=1, source_target_pairs={{0,1},{1,0},{2,3},{3,2},{4,5},{5,4},{6,7},{7,6},{8,9},{9,8},{10,11... | collective-permute-start | bytes 393224 | tf_op jit(solution)/shard_map/ppermute | solution.py:125
  115.5 11.5 %collective-permute-start.44 = (bf16[32,2048]{1,0:T(8,128)(2,1)S(1)}, bf16[32,2048]{1,0:T(8,128)(2,1)S(1)}, u32[]{:S(2)}, u32[]{:S(2)}) collective-permute-start(bf16[32,2048]{1,0:T(8,128)(2,1)S(1)} %get-tuple-element.73), channel_id=1, source_target_pairs={{0,16},{2,18},{4,20},{6,22},{8,24},{10,26},{12,28},{14,30},{16,0},... | collective-permute-start | bytes 393224 | tf_op jit(solution)/shard_map/ppermute | solution.py:122
  115.5 11.5 %collective-permute-start.43 = (bf16[32,2048]{1,0:T(8,128)(2,1)S(1)}, bf16[32,2048]{1,0:T(8,128)(2,1)S(1)}, u32[]{:S(2)}, u32[]{:S(2)}) collective-permute-start(bf16[32,2048]{1,0:T(8,128)(2,1)S(1)} %get-tuple-element.71), channel_id=1, source_target_pairs={{0,24},{2,26},{4,28},{6,30},{8,0},{10,2},{12,4},{14,6},{16,8},{18,... | collective-permute-start | bytes 393224 | tf_op jit(solution)/shard_map/ppermute | solution.py:122
  (25 other events, 156.4 us)
where the time goes:
time: 130 us; the launch traced here: 128 us
  starting transfers between devices  53.5 us (41%)
  waiting for transfers between devices  43.1 us (33%)
  Pallas kernels  22.2 us (17%)
  local copies, waits for them, and re-layouts  3.45 us (3%)
  other arithmetic  3.39 us (3%)
  between operations  2.16 us (2%)
    ppermute x42, waiting for transfers between devices, shift(): return lax.ppermute(value, 'row', pairs)  41.1 us
    ppermute x42, starting transfers between devices, shift(): return lax.ppermute(value, 'row', pairs)  39.3 us
    pallas_call x4, Pallas kernels, block_product(): pl.pallas_call(functools.partial(product_kernel, contract, outputs, n_in)...  22.2 us
    ppermute x4, starting transfers between devices, shift_col(): lax.ppermute(value, 'col', [(j, (j + d) % n_col) for j in range(n_col)])  14.1 us
    unnamed x6, local copies, waits for them, and re-layouts  3.39 us
  transfers between devices with their start and end apart: 46, of which 24 were waited for; matrix products, arithmetic and copies ran while one was open for 1% of the time, Pallas kernels for 17%

commit v1 on v0

--- a/solution.py
+++ b/solution.py
@@ -11,20 +11,17 @@
 UNROLL = 8
 
 
-def product_kernel(contract, outputs, n_in, count_ref, take_ref, put_ref, *refs):
+def product_kernel(contract, inputs, outputs, count_ref, take_ref, put_ref, *refs):
+    n_in = len(inputs)
     pieces = refs[:n_in]
     blocks = refs[n_in]
     outs = refs[n_in + 1 : n_in + 1 + len(outputs)]
-    held, held_blocks, total, piece_sems, block_sems = refs[n_in + 1 + len(outputs) :]
+    held, held_blocks, total, block_sems = refs[n_in + 1 + len(outputs) :]
     capacity, size_block = blocks.shape[0], blocks.shape[1]
     per_piece = held.shape[2] // size_block
     chunks = capacity // CHUNK
     count = count_ref[0]
 
-    copies = [pltpu.make_async_copy(pieces[p], held.at[p], piece_sems.at[p]) for p in range(n_in)]
-    for copy in copies:
-        copy.start()
-
     def block_copy(g):
         part = pl.ds(g * CHUNK, CHUNK)
         return pltpu.make_async_copy(blocks.at[part], held_blocks.at[part], block_sems.at[g])
@@ -35,8 +32,9 @@
             block_copy(g).start()
 
     total[...] = jnp.zeros_like(total)
-    for copy in copies:
-        copy.wait()
+    for part, held_pieces in zip(pieces, inputs):
+        for n, p in enumerate(held_pieces):
+            held[p] = part[n]
 
     def group(first):
         places = []
@@ -71,24 +69,25 @@
             out[n] = total[p].astype(out.dtype)
 
 
-def block_product(contract, outputs, dtypes, n_put, count, take, put, pieces, blocks):
+def block_product(contract, inputs, outputs, dtypes, n_put, count, take, put, pieces, blocks):
     capacity, size_block = blocks.shape[0], blocks.shape[1]
-    vector_count, own_rows = pieces[0].shape
-    n_in = len(pieces)
+    vector_count, own_rows = pieces[0].shape[-2:]
+    pieces = [part.reshape(-1, vector_count, own_rows) for part in pieces]
+    n_in = sum(part.shape[0] for part in pieces)
     smem = pl.BlockSpec(memory_space=pltpu.SMEM)
-    anywhere = pl.BlockSpec(memory_space=pl.ANY)
+    vmem = pl.BlockSpec(memory_space=pltpu.VMEM)
+    hbm = pl.BlockSpec(memory_space=pltpu.HBM)
     return pl.pallas_call(
-        functools.partial(product_kernel, contract, outputs, n_in),
+        functools.partial(product_kernel, contract, inputs, outputs),
         out_shape=[
             jax.ShapeDtypeStruct((len(held), vector_count, own_rows), dtype) for held, dtype in zip(outputs, dtypes)
         ],
-        in_specs=[smem] * 3 + [anywhere] * (n_in + 1),
+        in_specs=[smem] * 3 + [vmem] * len(pieces) + [hbm],
         out_specs=[pl.BlockSpec(memory_space=pltpu.VMEM)] * len(outputs),
         scratch_shapes=[
             pltpu.VMEM((n_in, vector_count, own_rows), jnp.bfloat16),
             pltpu.VMEM(blocks.shape, blocks.dtype),
             pltpu.VMEM((n_put + 1, vector_count, own_rows), jnp.float32),
-            pltpu.SemaphoreType.DMA((n_in,)),
             pltpu.SemaphoreType.DMA((capacity // CHUNK,)),
         ],
         compiler_params=pltpu.CompilerParams(vmem_limit_bytes=40 * 1024 * 1024),
@@ -98,7 +97,7 @@
             transcendentals=0,
         ),
         name="mirror" if contract == 0 else "forward",
-    )(count, take, put, *pieces, blocks)
+    )(count, take, put, *pieces, pltpu.with_memory_space_constraint(blocks, pltpu.HBM))
 
 
 def shards(n_row, n_col, vectors, block_values, block_rows, block_cols, block_counts, center, radius):
@@ -142,46 +141,55 @@
     put_cols = jnp.where(live, place_cols, n_row * per_piece)
     put_rows = jnp.where(live, place_rows, n_col * per_piece)
 
-    mirror_outputs = [
-        [piece(a, b, c) for a in range(n_a)] for c in range(n_c) for b in range(n_b)
-    ]
+    mirror_outputs = [[piece(a, b, c) for b in range(n_b) for a in range(n_a)] for c in range(n_c)]
     forward_outputs = [[j] for j in range(n_col)]
+    mirror_inputs = [[j] for j in range(n_col)]
+    forward_inputs = []
+    for c in range(n_c):
+        forward_inputs.append([piece(0, b, c) for b in range(n_b)] + [piece(a, 0, c) for a in range(1, n_a)])
+        if n_b > 1:
+            forward_inputs.append([piece(a, b, c) for b in range(1, n_b) for a in range(1, n_a)])
 
     def apply_operator(narrow):
         by_col = [narrow] + [shift_col(narrow, j) for j in range(1, n_col)]
-        along_a = [narrow] + [shift(narrow, da=a) for a in range(1, n_a)]
+        near = [narrow] + [shift(narrow, db=b) for b in range(1, n_b)]
+        far = [[shift(part, da=a) for a in range(1, n_a)] for part in near]
         mirrors = block_product(
-            0, mirror_outputs, [jnp.bfloat16] * len(mirror_outputs), n_row,
+            0, mirror_inputs, mirror_outputs, [jnp.bfloat16] * len(mirror_outputs), n_row,
             block_counts, place_rows, put_cols, by_col, block_values,
         )
-        along_a, mirrors = lax.optimization_barrier((along_a, mirrors))
-        along_b = list(along_a)
-        for b in range(1, n_b):
-            along_b += [shift(part, db=b) for part in along_a]
-        by_row = list(along_b)
+        far[0], mirrors = lax.optimization_barrier((far[0], mirrors))
+
+        shares = mirrors[0].astype(jnp.float32)
         for c in range(1, n_c):
-            by_row += [shift(part, dc=c) for part in along_b]
-
-        by_b = []
-        for b in range(n_b):
-            share = mirrors[b].astype(jnp.float32)
-            for c in range(1, n_c):
-                share += shift(mirrors[c * n_b + b], dc=-c).astype(jnp.float32)
-            by_b.append(share)
+            shares += shift(mirrors[c], dc=-c).astype(jnp.float32)
+        by_b = [shares[b * n_a : (b + 1) * n_a] for b in range(n_b)]
+        others = [shift(by_b[b].astype(jnp.bfloat16), db=-b) for b in range(1, n_b)]
+
+        early = jnp.stack(near + far[0])
+        late = [part for behind in far[1:] for part in behind]
+        late = [jnp.stack(late)] if late else []
+        by_row = [early] + late
+        for c in range(1, n_c):
+            by_row += [shift(part, dc=c) for part in [early] + late]
+        by_row, others = lax.optimization_barrier((by_row, others))
+
         share = by_b[0]
-        for b in range(1, n_b):
-            share += shift(by_b[b].astype(jnp.bfloat16), db=-b).astype(jnp.float32)
-        mirror_sum = share[0]
-        for a in range(1, n_a):
-            mirror_sum += shift(share[a].astype(jnp.bfloat16), da=-a).astype(jnp.float32)
+        for other in others:
+            share += other.astype(jnp.float32)
+        back = [shift(share[a].astype(jnp.bfloat16), da=-a) for a in range(1, n_a)]
 
         forwards = block_product(
-            1, forward_outputs, [jnp.float32] + [jnp.bfloat16] * (n_col - 1), n_col,
+            1, forward_inputs, forward_outputs, [jnp.float32] + [jnp.bfloat16] * (n_col - 1), n_col,
             block_counts, place_cols, put_rows, by_row, block_values,
         )
+        back, forwards = lax.optimization_barrier((back, forwards))
         forward_sum = forwards[0][0]
         for j in range(1, n_col):
             forward_sum += shift_col(forwards[j][0], -j).astype(jnp.float32)
+        mirror_sum = share[0]
+        for other in back:
+            mirror_sum += other.astype(jnp.float32)
         return forward_sum + mirror_sum
 
     current = (apply_operator(vectors.astype(jnp.bfloat16)) - center_value * vectors) / radius_value

time: 130 us -> 110 us (0.85)
  the two profiles are of different devices: /device:TPU:9 before, /device:TPU:0 now
where the time goes in v1:
time: 110 us; the launch traced here: 111 us
  waiting for transfers between devices  37.4 us (34%)
  Pallas kernels  36.6 us (33%)
  starting transfers between devices  30.9 us (28%)
  other arithmetic  3.79 us (3%)
  between operations  2.35 us (2%)
    pallas_call x4, Pallas kernels, block_product(): pl.pallas_call(functools.partial(product_kernel, contract, inputs, output...  36.6 us
    ppermute x28, starting transfers between devices, shift(): return lax.ppermute(value, 'row', pairs)  27.7 us
    ppermute x28, waiting for transfers between devices, shift(): return lax.ppermute(value, 'row', pairs)  26.4 us
    ppermute x4, waiting for transfers between devices, shift_col(): lax.ppermute(value, 'col', [(j, (j + d) % n_col) for j in range(n_col)])  10.9 us
    ppermute x4, starting transfers between devices, shift_col(): lax.ppermute(value, 'col', [(j, (j + d) % n_col) for j in range(n_col)])  3.22 us
  transfers between devices with their start and end apart: 32, of which 11 were waited for; matrix products, arithmetic and copies ran while one was open for 2% of the time, Pallas kernels for 33%

profile of v1, /device:TPU:0, one launch (start us, length us, event | category | flops | bytes accessed | tf_op | source)
XLA Modules:
  0.0 111.4 jit_solution(5804294575180127296)
XLA Ops:
  1.0 3.0 %collective-permute-start.3 = (bf16[32,2048]{1,0:T(8,128)(2,1)S(1)}, bf16[32,2048]{1,0:T(8,128)(2,1)S(1)}, u32[]{:S(2)}, u32[]{:S(2)}) collective-permute-start(bf16[32,2048]{1,0:T(8,128)(2,1)S(1)} %get-tuple-element.91), channel_id=1, source_target_pairs={{0,1},{1,0},{2,3},{3,2},{4,5},{5,4},{6,7},{7,6},{8,9},{9,8},{10,11... | collective-permute-start | bytes 393224 | tf_op jit(solution)/shard_map/ppermute | solution.py:124
  4.0 1.6 %collective-permute-start = (bf16[32,2048]{1,0:T(8,128)(2,1)S(1)}, bf16[32,2048]{1,0:T(8,128)(2,1)S(1)}, u32[]{:S(2)}, u32[]{:S(2)}) collective-permute-start(bf16[32,2048]{1,0:T(8,128)(2,1)S(1)} %get-tuple-element.91), channel_id=1, source_target_pairs={{0,8},{2,10},{4,12},{6,14},{8,16},{10,18},{12,20},{14,22},{16,24},... | collective-permute-start | bytes 393224 | tf_op jit(solution)/shard_map/ppermute | solution.py:121
  5.6 2.6 %collective-permute-start.1 = (bf16[32,2048]{1,0:T(8,128)(2,1)S(1)}, bf16[32,2048]{1,0:T(8,128)(2,1)S(1)}, u32[]{:S(2)}, u32[]{:S(2)}) collective-permute-start(bf16[32,2048]{1,0:T(8,128)(2,1)S(1)} %get-tuple-element.91), channel_id=1, source_target_pairs={{0,16},{2,18},{4,20},{6,22},{8,24},{10,26},{12,28},{14,30},{16,0},... | collective-permute-start | bytes 393224 | tf_op jit(solution)/shard_map/ppermute | solution.py:121
  9.5 1.5 %collective-permute-start.5 = (bf16[32,2048]{1,0:T(8,128)(2,1)S(1)}, bf16[32,2048]{1,0:T(8,128)(2,1)S(1)}, u32[]{:S(2)}, u32[]{:S(2)}) collective-permute-start(bf16[32,2048]{1,0:T(8,128)(2,1)S(1)} %get-tuple-element.91), channel_id=1, source_target_pairs={{0,4},{2,6},{4,0},{6,2},{8,12},{10,14},{12,8},{14,10},{16,20},{18,... | collective-permute-start | bytes 393224 | tf_op jit(solution)/shard_map/ppermute | solution.py:121
  12.4 8.2 %mirror.2 = (bf16[8,32,2048]{2,1,0:T(8,128)(2,1)S(1)}, bf16[8,32,2048]{2,1,0:T(8,128)(2,1)S(1)}) custom-call(s32[1]{0:T(128)} %copy.16.count_ref, s32[256]{0:T(256)S(1)} %get-tuple-element.87.take_ref, s32[256]{0:T(256)S(1)} %get-tuple-element.100.put_ref, bf16[1,32,2048]{2,1,0:T(8,128)(2,1)S(1)} %bitcast.93, bf16[1,32,2048]{2,1,0:T(8,128)(2,1)S(1)} %bitcast.94, ...), custom_call_target="tpu_custom_call" | custom-call | flops 2147483648 | bytes 8650752 | tf_op jit(solution)/shard_map/mirror/pallas_call | solution.py:80
  22.1 3.1 %collective-permute-start.8 = (bf16[32,2048]{1,0:T(8,128)(2,1)S(1)}, bf16[32,2048]{1,0:T(8,128)(2,1)S(1)}, u32[]{:S(2)}, u32[]{:S(2)}) collective-permute-start(bf16[32,2048]{1,0:T(8,128)(2,1)S(1)} %collective-permute-done.5), channel_id=1, source_target_pairs={{0,24},{2,26},{4,28},{6,30},{8,0},{10,2},{12,4},{14,6},{16,8},{18,... | collective-permute-start | bytes 393224 | tf_op jit(solution)/shard_map/ppermute | solution.py:121
  25.7 3.9 %collective-permute-done.6 = bf16[32,2048]{1,0:T(8,128)(2,1)S(1)} collective-permute-done((bf16[32,2048]{1,0:T(8,128)(2,1)S(1)}, bf16[32,2048]{1,0:T(8,128)(2,1)S(1)}, u32[]{:S(2)}, u32[]{:S(2)}) %collective-permute-start.6) | collective-permute-done | bytes 131104 | tf_op jit(solution)/shard_map/ppermute | solution.py:121
  29.7 4.6 %collective-permute-done.7 = bf16[32,2048]{1,0:T(8,128)(2,1)S(1)} collective-permute-done((bf16[32,2048]{1,0:T(8,128)(2,1)S(1)}, bf16[32,2048]{1,0:T(8,128)(2,1)S(1)}, u32[]{:S(2)}, u32[]{:S(2)}) %collective-permute-start.7) | collective-permute-done | bytes 131104 | tf_op jit(solution)/shard_map/ppermute | solution.py:121
  34.4 1.7 %collective-permute-done.10.refs_3_ = bf16[3,32,2048]{2,1,0:T(8,128)(2,1)S(1)} collective-permute-done((bf16[3,32,2048]{2,1,0:T(8,128)(2,1)S(1)}, bf16[3,32,2048]{2,1,0:T(8,128)(2,1)S(1)}, u32[]{:S(2)}, u32[]{:S(2)}) %collective-permute-start.10) | collective-permute-done | bytes 393248 | tf_op jit(solution)/shard_map/ppermute | solution.py:121
  36.1 2.9 %collective-permute-done.11 = bf16[4,32,2048]{2,1,0:T(8,128)(2,1)S(1)} collective-permute-done((bf16[4,32,2048]{2,1,0:T(8,128)(2,1)S(1)}, bf16[4,32,2048]{2,1,0:T(8,128)(2,1)S(1)}, u32[]{:S(2)}, u32[]{:S(2)}) %collective-permute-start.11) | collective-permute-done | bytes 524320 | tf_op jit(solution)/shard_map/ppermute | solution.py:121
  41.3 1.7 %collective-permute-start.14 = (bf16[32,2048]{1,0:T(8,128)(2,1)S(1)}, bf16[32,2048]{1,0:T(8,128)(2,1)S(1)}, u32[]{:S(2)}, u32[]{:S(2)}) collective-permute-start(bf16[32,2048]{1,0:T(8,128)(2,1)S(1)} %get-tuple-element.97), channel_id=1, source_target_pairs={{0,8},{2,10},{4,12},{6,14},{8,16},{10,18},{12,20},{14,22},{16,24},... | collective-permute-start | bytes 393224 | tf_op jit(solution)/shard_map/ppermute | solution.py:121
  43.1 10.1 %forward.2 = (f32[1,32,2048]{2,1,0:T(8,128)S(1)}, bf16[1,32,2048]{2,1,0:T(8,128)(2,1)S(1)}) custom-call(s32[1]{0:T(128)} %copy.16.count_ref, s32[256]{0:T(256)S(1)} %get-tuple-element.101.take_ref, s32[256]{0:T(256)S(1)} %get-tuple-element.86.put_ref, bf16[5,32,2048]{2,1,0:T(8,128)(2,1)S(1)} %bitcast_dynamic-update-slice_fusion.4.refs_0_, ...), custom_call_target="tpu_custom_call" | custom-call | flops 2147483648 | bytes 10485760 | tf_op jit(solution)/shard_map/forward/pallas_call | solution.py:80
  54.6 4.9 %collective-permute-done.15 = bf16[32,2048]{1,0:T(8,128)(2,1)S(1)} collective-permute-done((bf16[32,2048]{1,0:T(8,128)(2,1)S(1)}, bf16[32,2048]{1,0:T(8,128)(2,1)S(1)}, u32[]{:S(2)}, u32[]{:S(2)}) %collective-permute-start.15) | collective-permute-done | bytes 131104 | tf_op jit(solution)/shard_map/ppermute | solution.py:124
  59.9 3.7 %collective-permute-start.18 = (bf16[32,2048]{1,0:T(8,128)(2,1)S(1)}, bf16[32,2048]{1,0:T(8,128)(2,1)S(1)}, u32[]{:S(2)}, u32[]{:S(2)}) collective-permute-start(bf16[32,2048]{1,0:T(8,128)(2,1)S(1)} %get-tuple-element.84), channel_id=1, source_target_pairs={{0,24},{2,26},{4,28},{6,30},{8,0},{10,2},{12,4},{14,6},{16,8},{18,... | collective-permute-start | bytes 393224 | tf_op jit(solution)/shard_map/ppermute | solution.py:121
  64.7 8.2 %mirror.3 = (bf16[8,32,2048]{2,1,0:T(8,128)(2,1)S(1)}, bf16[8,32,2048]{2,1,0:T(8,128)(2,1)S(1)}) custom-call(s32[1]{0:T(128)} %copy.16.count_ref, s32[256]{0:T(256)S(1)} %get-tuple-element.87.take_ref, s32[256]{0:T(256)S(1)} %get-tuple-element.100.put_ref, bf16[1,32,2048]{2,1,0:T(8,128)(2,1)S(1)} %bitcast.92, bf16[1,32,2048]{2,1,0:T(8,128)(2,1)S(1)} %bitcast.95, ...), custom_call_target="tpu_custom_call" | custom-call | flops 2147483648 | bytes 8650752 | tf_op jit(solution)/shard_map/mirror/pallas_call | solution.py:80
  74.9 2.6 %collective-permute-start.24 = (bf16[32,2048]{1,0:T(8,128)(2,1)S(1)}, bf16[32,2048]{1,0:T(8,128)(2,1)S(1)}, u32[]{:S(2)}, u32[]{:S(2)}) collective-permute-start(bf16[32,2048]{1,0:T(8,128)(2,1)S(1)} %collective-permute-done.21), channel_id=1, source_target_pairs={{0,24},{2,26},{4,28},{6,30},{8,0},{10,2},{12,4},{14,6},{16,8},{18,... | collective-permute-start | bytes 393224 | tf_op jit(solution)/shard_map/ppermute | solution.py:121
  78.0 3.9 %collective-permute-done.22 = bf16[32,2048]{1,0:T(8,128)(2,1)S(1)} collective-permute-done((bf16[32,2048]{1,0:T(8,128)(2,1)S(1)}, bf16[32,2048]{1,0:T(8,128)(2,1)S(1)}, u32[]{:S(2)}, u32[]{:S(2)}) %collective-permute-start.22) | collective-permute-done | bytes 131104 | tf_op jit(solution)/shard_map/ppermute | solution.py:121
  81.9 4.6 %collective-permute-done.23 = bf16[32,2048]{1,0:T(8,128)(2,1)S(1)} collective-permute-done((bf16[32,2048]{1,0:T(8,128)(2,1)S(1)}, bf16[32,2048]{1,0:T(8,128)(2,1)S(1)}, u32[]{:S(2)}, u32[]{:S(2)}) %collective-permute-start.23) | collective-permute-done | bytes 131104 | tf_op jit(solution)/shard_map/ppermute | solution.py:121
  86.7 1.7 %collective-permute-done.26.refs_3_ = bf16[3,32,2048]{2,1,0:T(8,128)(2,1)S(1)} collective-permute-done((bf16[3,32,2048]{2,1,0:T(8,128)(2,1)S(1)}, bf16[3,32,2048]{2,1,0:T(8,128)(2,1)S(1)}, u32[]{:S(2)}, u32[]{:S(2)}) %collective-permute-start.26) | collective-permute-done | bytes 393248 | tf_op jit(solution)/shard_map/ppermute | solution.py:121
  88.4 2.9 %collective-permute-done.27 = bf16[4,32,2048]{2,1,0:T(8,128)(2,1)S(1)} collective-permute-done((bf16[4,32,2048]{2,1,0:T(8,128)(2,1)S(1)}, bf16[4,32,2048]{2,1,0:T(8,128)(2,1)S(1)}, u32[]{:S(2)}, u32[]{:S(2)}) %collective-permute-start.27) | collective-permute-done | bytes 524320 | tf_op jit(solution)/shard_map/ppermute | solution.py:121
  92.2 1.4 %collective-permute-start.29 = (bf16[32,2048]{1,0:T(8,128)(2,1)S(1)}, bf16[32,2048]{1,0:T(8,128)(2,1)S(1)}, u32[]{:S(2)}, u32[]{:S(2)}) collective-permute-start(bf16[32,2048]{1,0:T(8,128)(2,1)S(1)} %get-tuple-element.95), channel_id=1, source_target_pairs={{0,16},{2,18},{4,20},{6,22},{8,24},{10,26},{12,28},{14,30},{16,0},... | collective-permute-start | bytes 393224 | tf_op jit(solution)/shard_map/ppermute | solution.py:121
  93.6 1.7 %collective-permute-start.30 = (bf16[32,2048]{1,0:T(8,128)(2,1)S(1)}, bf16[32,2048]{1,0:T(8,128)(2,1)S(1)}, u32[]{:S(2)}, u32[]{:S(2)}) collective-permute-start(bf16[32,2048]{1,0:T(8,128)(2,1)S(1)} %get-tuple-element.94), channel_id=1, source_target_pairs={{0,8},{2,10},{4,12},{6,14},{8,16},{10,18},{12,20},{14,22},{16,24},... | collective-permute-start | bytes 393224 | tf_op jit(solution)/shard_map/ppermute | solution.py:121
  95.3 10.1 %forward.3 = (f32[1,32,2048]{2,1,0:T(8,128)S(1)}, bf16[1,32,2048]{2,1,0:T(8,128)(2,1)S(1)}) custom-call(s32[1]{0:T(128)} %copy.16.count_ref, s32[256]{0:T(256)S(1)} %get-tuple-element.101.take_ref, s32[256]{0:T(256)S(1)} %get-tuple-element.86.put_ref, bf16[5,32,2048]{2,1,0:T(8,128)(2,1)S(1)} %bitcast_dynamic-update-slice_fusion.refs_0_, ...), custom_call_target="tpu_custom_call" | custom-call | flops 2147483648 | bytes 10485760 | tf_op jit(solution)/shard_map/forward/pallas_call | solution.py:80
  105.6 5.0 %collective-permute-done.31 = bf16[32,2048]{1,0:T(8,128)(2,1)S(1)} collective-permute-done((bf16[32,2048]{1,0:T(8,128)(2,1)S(1)}, bf16[32,2048]{1,0:T(8,128)(2,1)S(1)}, u32[]{:S(2)}, u32[]{:S(2)}) %collective-permute-start.31) | collective-permute-done | bytes 131104 | tf_op jit(solution)/shard_map/ppermute | solution.py:124
  (68 shorter events, 13.1 us)
Async XLA Ops:
  1.0 11.4 %collective-permute-start.3 = (bf16[32,2048]{1,0:T(8,128)(2,1)S(1)}, bf16[32,2048]{1,0:T(8,128)(2,1)S(1)}, u32[]{:S(2)}, u32[]{:S(2)}) collective-permute-start(bf16[32,2048]{1,0:T(8,128)(2,1)S(1)} %get-tuple-element.91), channel_id=1, source_target_pairs={{0,1},{1,0},{2,3},{3,2},{4,5},{5,4},{6,7},{7,6},{8,9},{9,8},{10,11... | collective-permute-start | bytes 393224 | tf_op jit(solution)/shard_map/ppermute | solution.py:124
  4.0 16.7 %collective-permute-start = (bf16[32,2048]{1,0:T(8,128)(2,1)S(1)}, bf16[32,2048]{1,0:T(8,128)(2,1)S(1)}, u32[]{:S(2)}, u32[]{:S(2)}) collective-permute-start(bf16[32,2048]{1,0:T(8,128)(2,1)S(1)} %get-tuple-element.91), channel_id=1, source_target_pairs={{0,8},{2,10},{4,12},{6,14},{8,16},{10,18},{12,20},{14,22},{16,24},... | collective-permute-start | bytes 393224 | tf_op jit(solution)/shard_map/ppermute | solution.py:121
  5.6 15.1 %collective-permute-start.1 = (bf16[32,2048]{1,0:T(8,128)(2,1)S(1)}, bf16[32,2048]{1,0:T(8,128)(2,1)S(1)}, u32[]{:S(2)}, u32[]{:S(2)}) collective-permute-start(bf16[32,2048]{1,0:T(8,128)(2,1)S(1)} %get-tuple-element.91), channel_id=1, source_target_pairs={{0,16},{2,18},{4,20},{6,22},{8,24},{10,26},{12,28},{14,30},{16,0},... | collective-permute-start | bytes 393224 | tf_op jit(solution)/shard_map/ppermute | solution.py:121
  8.1 12.5 %collective-permute-start.2 = (bf16[32,2048]{1,0:T(8,128)(2,1)S(1)}, bf16[32,2048]{1,0:T(8,128)(2,1)S(1)}, u32[]{:S(2)}, u32[]{:S(2)}) collective-permute-start(bf16[32,2048]{1,0:T(8,128)(2,1)S(1)} %get-tuple-element.91), channel_id=1, source_target_pairs={{0,24},{2,26},{4,28},{6,30},{8,0},{10,2},{12,4},{14,6},{16,8},{18,... | collective-permute-start | bytes 393224 | tf_op jit(solution)/shard_map/ppermute | solution.py:121
  9.5 11.3 %collective-permute-start.5 = (bf16[32,2048]{1,0:T(8,128)(2,1)S(1)}, bf16[32,2048]{1,0:T(8,128)(2,1)S(1)}, u32[]{:S(2)}, u32[]{:S(2)}) collective-permute-start(bf16[32,2048]{1,0:T(8,128)(2,1)S(1)} %get-tuple-element.91), channel_id=1, source_target_pairs={{0,4},{2,6},{4,0},{6,2},{8,12},{10,14},{12,8},{14,10},{16,20},{18,... | collective-permute-start | bytes 393224 | tf_op jit(solution)/shard_map/ppermute | solution.py:121
  20.8 15.3 %collective-permute-start.9 = (bf16[5,32,2048]{2,1,0:T(8,128)(2,1)S(1)}, bf16[5,32,2048]{2,1,0:T(8,128)(2,1)S(1)}, u32[]{:S(2)}, u32[]{:S(2)}) collective-permute-start(bf16[5,32,2048]{2,1,0:T(8,128)(2,1)S(1)} %bitcast_dynamic-update-slice_fusion.4.refs_0_), channel_id=1, source_target_pairs={{0,2},{2,0},{4,6},{6,4},{8,10},{10,8},{12,14},{14,12},{16,18},{18,... | collective-permute-start | bytes 1966088 | tf_op jit(solution)/shard_map/ppermute | solution.py:121
  21.4 8.3 %collective-permute-start.6 = (bf16[32,2048]{1,0:T(8,128)(2,1)S(1)}, bf16[32,2048]{1,0:T(8,128)(2,1)S(1)}, u32[]{:S(2)}, u32[]{:S(2)}) collective-permute-start(bf16[32,2048]{1,0:T(8,128)(2,1)S(1)} %collective-permute-done.5), channel_id=1, source_target_pairs={{0,8},{2,10},{4,12},{6,14},{8,16},{10,18},{12,20},{14,22},{16,24},... | collective-permute-start | bytes 393224 | tf_op jit(solution)/shard_map/ppermute | solution.py:121
  21.4 12.9 %collective-permute-start.7 = (bf16[32,2048]{1,0:T(8,128)(2,1)S(1)}, bf16[32,2048]{1,0:T(8,128)(2,1)S(1)}, u32[]{:S(2)}, u32[]{:S(2)}) collective-permute-start(bf16[32,2048]{1,0:T(8,128)(2,1)S(1)} %collective-permute-done.5), channel_id=1, source_target_pairs={{0,16},{2,18},{4,20},{6,22},{8,24},{10,26},{12,28},{14,30},{16,0},... | collective-permute-start | bytes 393224 | tf_op jit(solution)/shard_map/ppermute | solution.py:121
  22.1 12.2 %collective-permute-start.8 = (bf16[32,2048]{1,0:T(8,128)(2,1)S(1)}, bf16[32,2048]{1,0:T(8,128)(2,1)S(1)}, u32[]{:S(2)}, u32[]{:S(2)}) collective-permute-start(bf16[32,2048]{1,0:T(8,128)(2,1)S(1)} %collective-permute-done.5), channel_id=1, source_target_pairs={{0,24},{2,26},{4,28},{6,30},{8,0},{10,2},{12,4},{14,6},{16,8},{18,... | collective-permute-start | bytes 393224 | tf_op jit(solution)/shard_map/ppermute | solution.py:121
  25.6 13.4 %collective-permute-start.11 = (bf16[4,32,2048]{2,1,0:T(8,128)(2,1)S(1)}, bf16[4,32,2048]{2,1,0:T(8,128)(2,1)S(1)}, u32[]{:S(2)}, u32[]{:S(2)}) collective-permute-start(bf16[4,32,2048]{2,1,0:T(8,128)(2,1)S(1)} %slice.109), channel_id=1, source_target_pairs={{0,4},{2,6},{4,0},{6,2},{8,12},{10,14},{12,8},{14,10},{16,20},{18,... | collective-permute-start | bytes 1572872 | tf_op jit(solution)/shard_map/ppermute | solution.py:121
  39.3 13.9 %collective-permute-start.12 = (bf16[32,2048]{1,0:T(8,128)(2,1)S(1)}, bf16[32,2048]{1,0:T(8,128)(2,1)S(1)}, u32[]{:S(2)}, u32[]{:S(2)}) collective-permute-start(bf16[32,2048]{1,0:T(8,128)(2,1)S(1)} %get-tuple-element.99), channel_id=1, source_target_pairs={{0,24},{2,26},{4,28},{6,30},{8,0},{10,2},{12,4},{14,6},{16,8},{18,... | collective-permute-start | bytes 393224 | tf_op jit(solution)/shard_map/ppermute | solution.py:121
  39.9 13.3 %collective-permute-start.13 = (bf16[32,2048]{1,0:T(8,128)(2,1)S(1)}, bf16[32,2048]{1,0:T(8,128)(2,1)S(1)}, u32[]{:S(2)}, u32[]{:S(2)}) collective-permute-start(bf16[32,2048]{1,0:T(8,128)(2,1)S(1)} %get-tuple-element.98), channel_id=1, source_target_pairs={{0,16},{2,18},{4,20},{6,22},{8,24},{10,26},{12,28},{14,30},{16,0},... | collective-permute-start | bytes 393224 | tf_op jit(solution)/shard_map/ppermute | solution.py:121
  41.3 11.9 %collective-permute-start.14 = (bf16[32,2048]{1,0:T(8,128)(2,1)S(1)}, bf16[32,2048]{1,0:T(8,128)(2,1)S(1)}, u32[]{:S(2)}, u32[]{:S(2)}) collective-permute-start(bf16[32,2048]{1,0:T(8,128)(2,1)S(1)} %get-tuple-element.97), channel_id=1, source_target_pairs={{0,8},{2,10},{4,12},{6,14},{8,16},{10,18},{12,20},{14,22},{16,24},... | collective-permute-start | bytes 393224 | tf_op jit(solution)/shard_map/ppermute | solution.py:121
  59.7 13.2 %collective-permute-start.16 = (bf16[32,2048]{1,0:T(8,128)(2,1)S(1)}, bf16[32,2048]{1,0:T(8,128)(2,1)S(1)}, u32[]{:S(2)}, u32[]{:S(2)}) collective-permute-start(bf16[32,2048]{1,0:T(8,128)(2,1)S(1)} %get-tuple-element.84), channel_id=1, source_target_pairs={{0,8},{2,10},{4,12},{6,14},{8,16},{10,18},{12,20},{14,22},{16,24},... | collective-permute-start | bytes 393224 | tf_op jit(solution)/shard_map/ppermute | solution.py:121
  59.8 13.1 %collective-permute-start.17 = (bf16[32,2048]{1,0:T(8,128)(2,1)S(1)}, bf16[32,2048]{1,0:T(8,128)(2,1)S(1)}, u32[]{:S(2)}, u32[]{:S(2)}) collective-permute-start(bf16[32,2048]{1,0:T(8,128)(2,1)S(1)} %get-tuple-element.84), channel_id=1, source_target_pairs={{0,16},{2,18},{4,20},{6,22},{8,24},{10,26},{12,28},{14,30},{16,0},... | collective-permute-start | bytes 393224 | tf_op jit(solution)/shard_map/ppermute | solution.py:121
  59.9 13.0 %collective-permute-start.18 = (bf16[32,2048]{1,0:T(8,128)(2,1)S(1)}, bf16[32,2048]{1,0:T(8,128)(2,1)S(1)}, u32[]{:S(2)}, u32[]{:S(2)}) collective-permute-start(bf16[32,2048]{1,0:T(8,128)(2,1)S(1)} %get-tuple-element.84), channel_id=1, source_target_pairs={{0,24},{2,26},{4,28},{6,30},{8,0},{10,2},{12,4},{14,6},{16,8},{18,... | collective-permute-start | bytes 393224 | tf_op jit(solution)/shard_map/ppermute | solution.py:121
  63.6 9.4 %collective-permute-start.21 = (bf16[32,2048]{1,0:T(8,128)(2,1)S(1)}, bf16[32,2048]{1,0:T(8,128)(2,1)S(1)}, u32[]{:S(2)}, u32[]{:S(2)}) collective-permute-start(bf16[32,2048]{1,0:T(8,128)(2,1)S(1)} %get-tuple-element.84), channel_id=1, source_target_pairs={{0,4},{2,6},{4,0},{6,2},{8,12},{10,14},{12,8},{14,10},{16,20},{18,... | collective-permute-start | bytes 393224 | tf_op jit(solution)/shard_map/ppermute | solution.py:121
  73.1 15.3 %collective-permute-start.25 = (bf16[5,32,2048]{2,1,0:T(8,128)(2,1)S(1)}, bf16[5,32,2048]{2,1,0:T(8,128)(2,1)S(1)}, u32[]{:S(2)}, u32[]{:S(2)}) collective-permute-start(bf16[5,32,2048]{2,1,0:T(8,128)(2,1)S(1)} %bitcast_dynamic-update-slice_fusion.refs_0_), channel_id=1, source_target_pairs={{0,2},{2,0},{4,6},{6,4},{8,10},{10,8},{12,14},{14,12},{16,18},{18,... | collective-permute-start | bytes 1966088 | tf_op jit(solution)/shard_map/ppermute | solution.py:121
  73.6 12.9 %collective-permute-start.23 = (bf16[32,2048]{1,0:T(8,128)(2,1)S(1)}, bf16[32,2048]{1,0:T(8,128)(2,1)S(1)}, u32[]{:S(2)}, u32[]{:S(2)}) collective-permute-start(bf16[32,2048]{1,0:T(8,128)(2,1)S(1)} %collective-permute-done.21), channel_id=1, source_target_pairs={{0,16},{2,18},{4,20},{6,22},{8,24},{10,26},{12,28},{14,30},{16,0},... | collective-permute-start | bytes 393224 | tf_op jit(solution)/shard_map/ppermute | solution.py:121
  74.9 11.6 %collective-permute-start.24 = (bf16[32,2048]{1,0:T(8,128)(2,1)S(1)}, bf16[32,2048]{1,0:T(8,128)(2,1)S(1)}, u32[]{:S(2)}, u32[]{:S(2)}) collective-permute-start(bf16[32,2048]{1,0:T(8,128)(2,1)S(1)} %collective-permute-done.21), channel_id=1, source_target_pairs={{0,24},{2,26},{4,28},{6,30},{8,0},{10,2},{12,4},{14,6},{16,8},{18,... | collective-permute-start | bytes 393224 | tf_op jit(solution)/shard_map/ppermute | solution.py:121
  77.9 13.4 %collective-permute-start.27 = (bf16[4,32,2048]{2,1,0:T(8,128)(2,1)S(1)}, bf16[4,32,2048]{2,1,0:T(8,128)(2,1)S(1)}, u32[]{:S(2)}, u32[]{:S(2)}) collective-permute-start(bf16[4,32,2048]{2,1,0:T(8,128)(2,1)S(1)} %slice.108), channel_id=1, source_target_pairs={{0,4},{2,6},{4,0},{6,2},{8,12},{10,14},{12,8},{14,10},{16,20},{18,... | collective-permute-start | bytes 1572872 | tf_op jit(solution)/shard_map/ppermute | solution.py:121
  91.5 13.9 %collective-permute-start.28 = (bf16[32,2048]{1,0:T(8,128)(2,1)S(1)}, bf16[32,2048]{1,0:T(8,128)(2,1)S(1)}, u32[]{:S(2)}, u32[]{:S(2)}) collective-permute-start(bf16[32,2048]{1,0:T(8,128)(2,1)S(1)} %get-tuple-element.96), channel_id=1, source_target_pairs={{0,24},{2,26},{4,28},{6,30},{8,0},{10,2},{12,4},{14,6},{16,8},{18,... | collective-permute-start | bytes 393224 | tf_op jit(solution)/shard_map/ppermute | solution.py:121
  92.2 13.3 %collective-permute-start.29 = (bf16[32,2048]{1,0:T(8,128)(2,1)S(1)}, bf16[32,2048]{1,0:T(8,128)(2,1)S(1)}, u32[]{:S(2)}, u32[]{:S(2)}) collective-permute-start(bf16[32,2048]{1,0:T(8,128)(2,1)S(1)} %get-tuple-element.95), channel_id=1, source_target_pairs={{0,16},{2,18},{4,20},{6,22},{8,24},{10,26},{12,28},{14,30},{16,0},... | collective-permute-start | bytes 393224 | tf_op jit(solution)/shard_map/ppermute | solution.py:121
  93.6 11.9 %collective-permute-start.30 = (bf16[32,2048]{1,0:T(8,128)(2,1)S(1)}, bf16[32,2048]{1,0:T(8,128)(2,1)S(1)}, u32[]{:S(2)}, u32[]{:S(2)}) collective-permute-start(bf16[32,2048]{1,0:T(8,128)(2,1)S(1)} %get-tuple-element.94), channel_id=1, source_target_pairs={{0,8},{2,10},{4,12},{6,14},{8,16},{10,18},{12,20},{14,22},{16,24},... | collective-permute-start | bytes 393224 | tf_op jit(solution)/shard_map/ppermute | solution.py:121
  (9 other events, 53.7 us)
